TPU v7x, 32 devices: a whole 2x2x4 slice. The times are simulated.
32 devices in a mesh: groups: 2 (over x), patch: 16 (over z, y, core).
Axes of the slice: x: 2, y: 2, z: 4, core: 2. Of those that a mesh axis runs over, the one named last changes fastest.
Arguments:
- trial: float32 [64, 262144], P('groups', 'patch'), parts along dimension 0
- loads: float32 [8, 262144], P(None, 'patch'), may hold values from -6 to 6
- band: float32 [9, 262144], P(None, 'patch'), may hold values from -3 to 3
- seeds: int32 [64], P('groups'), parts along dimension 0, may hold values from 0 to 7
- iface_rows: int32 [2048], P('patch'), may hold values from 0 to 16383, as said below
- iface_partner: int32 [2048], P('patch'), may hold values from 0 to 2047
- patch_device: int32 [16], replicated, may hold values from 0 to 15, as said below
- iface_weight: float32 [2048], P('patch'), may hold values from 0.5 to 1.5
Outputs:
- r_factor: float32 [64, 32], P('groups'), parts along dimension 0
- basis: float32 [64, 262144], P('groups', 'patch'), parts along dimension 0
There are 2 independent parts, one for each index of `groups`. A program takes and returns all parts, laid end to end along the dimension named above; an argument that names none is the same for every part. Nothing has to cross between parts.
Inputs may be any that keep to these rules, and one draw needn't show every extreme that they name: `iface_rows`: the 128 slots of one device name distinct local unknowns, among them 0 and 16383. `patch_device`: A permutation of the patches.
All inputs are finite; a program needn't handle non-finite values.
Results may differ from a plain program's by a relative error of at most 0.00005.
Values sent between devices are 32-bit elements; how exact they have to be, the bound alone decides.
A program may use at most 64 MiB of HBM per device.

v0:
```python
import jax
import jax.numpy as jnp
from jax import lax
from jax.sharding import PartitionSpec as P


def padded_2(cells, sides, width):
    for axis, dim in sides:
        count = lax.axis_size(axis)
        head = lax.slice_in_dim(cells, 0, width, axis=dim)
        tail = lax.slice_in_dim(cells, cells.shape[dim] - width, cells.shape[dim], axis=dim)
        cells = jnp.concatenate(
            [
                lax.ppermute(tail, axis, [(i, (i + 1) % count) for i in range(count)]),
                cells,
                lax.ppermute(head, axis, [((i + 1) % count, i) for i in range(count)]),
            ],
            axis=dim,
        )
    return cells


def per_device(trial, loads, band, seeds, iface_rows, iface_partner, patch_device, iface_weight):
    snap_count, rows = trial.shape
    slot_count = iface_rows.shape[0]
    half_slots = slot_count // 2
    width = band.shape[0]
    half = (width - 1) // 2
    values = trial[:, iface_rows]
    partner_slot = iface_partner % slot_count
    arranged = jnp.concatenate([values[:, half_slots:], values[:, :half_slots]], axis=1)
    extended = padded_2(arranged, (("patch", 1),), half_slots)
    local_ids = jnp.arange(slot_count, dtype=jnp.int32)
    where_ids = jnp.where(local_ids < half_slots, slot_count + partner_slot, partner_slot)
    coupled_raw = extended[:, where_ids]
    coupled = coupled_raw * iface_weight[None, :]
    padded = jnp.pad(trial, ((0, 0), (half, half)))
    banded = jnp.zeros((snap_count, rows), jnp.float32)
    for shift_k in range(width):
        banded = banded + band[shift_k][None, :] * padded[:, shift_k : shift_k + rows]
    pattern_ids = jnp.arange(loads.shape[0], dtype=jnp.int32)
    one_hot = (seeds[:, None] == pattern_ids[None, :]).astype(jnp.float32)
    chosen = jnp.dot(
        one_hot, loads, preferred_element_type=jnp.float32, precision=lax.Precision.HIGHEST
    )
    snapshots = (chosen - banded).at[:, iface_rows].add(coupled)
    local_gram = jnp.dot(
        snapshots, snapshots.T, preferred_element_type=jnp.float32, precision=lax.Precision.HIGHEST
    )
    lower = jnp.linalg.cholesky(lax.psum(local_gram, "patch"))
    scale = jnp.sqrt(jnp.float32(rows * lax.axis_size("patch")))
    basis = lax.linalg.triangular_solve(lower, snapshots, left_side=True, lower=True) * scale
    return (lower.T / scale, basis)


def solution(mesh):
    placed = (
        P("groups", "patch"),
        P(None, "patch"),
        P(None, "patch"),
        P("groups"),
        P("patch"),
        P("patch"),
        P(),
        P("patch"),
    )
    return jax.shard_map(
        per_device,
        mesh=mesh,
        in_specs=placed,
        out_specs=(P("groups", None), P("groups", "patch")),
        check_vma=False,
    )
```

profile of v0, /device:TPU:0, one launch (start us, length us, event | category | flops | bytes accessed | tf_op | source)
XLA Modules:
  0.0 137.8 jit_solution(14990107829892304772)
XLA Ops:
  0.6 0.0 copy-start
  0.6 0.7 compare_select_fusion.1
  1.4 0.0 copy-start.3
  1.4 0.0 copy-start.1
  1.4 0.0 copy-start.4
  1.4 6.4 %copy.24 = f32[32,16384]{0,1:T(8,128)} copy(f32[32,16384]{1,0:T(8,128)} %param.8) | data formatting | bytes 4194304 | tf_op args[0]
  7.8 4.0 %gather_fusion = f32[128,32]{1,0:T(8,128)S(1)} fusion(f32[32,16384]{0,1:T(8,128)} %copy.24, s32[1024]{0:T(1024)S(1)} %pad_clamp_fusion.1), kind=kCustom, calls=%fused_computation | custom fusion | bytes 33280 | tf_op jit(solution)/shard_map/gather | solution.py:29
  11.8 0.5 collective-permute-start
  12.3 5.1 %collective-permute-start.1 = (f32[32,64]{0,1:T(8,128)S(1)}, f32[32,64]{0,1:T(8,128)S(1)}, u32[]{:S(2)}, u32[]{:S(2)}) collective-permute-start(f32[32,64]{0,1:T(8,128)S(1)} %get-tuple-element.18), channel_id=1, source_target_pairs={{1,0},{2,1},{3,2},{4,3},{5,4},{6,5},{7,6},{8,7},{9,8},{10,9},{11,1... | collective-permute-start | bytes 24584 | tf_op jit(solution)/shard_map/ppermute | solution.py:16
  17.4 0.0 copy-done.3
  17.4 3.7 %fusion.13 = (f32[1,16384]{1,0:T(1,128)S(1)}, f32[1,16384]{1,0:T(1,128)S(1)}, f32[1,16384]{1,0:T(1,128)S(1)}, f32[1,16384]{1,0:T(1,128)S(1)}, f32[1,16384]{1,0:T...) fusion(f32[9,16384]{1,0:T(8,128)} %param.10), kind=kLoop, calls=%fused_computation.39 | loop fusion | bytes 1179648 | tf_op jit(solution)/shard_map/slice | solution.py:40
  21.1 0.0 copy-done
  21.1 0.0 copy-done.1
  21.1 0.0 copy-done.4
  21.1 5.7 %convolution_subtract_fusion = f32[32,16384]{1,0:T(8,128)} fusion(f32[8,16384]{1,0:T(8,128)S(1)} %copy-done, f32[32,16384]{1,0:T(8,128)S(1)} %copy-done.1, f32[16384]{0:T(1024)S(1)} %bitcast.33, f32[16384]{0:T(1024)S(1)} %bitcast.34, f32[16384]{0:T(1024)S(1)} %bitcast.27, f32[16384]{0:T(1024)S(1)} %bitcast.28, f32[16384]{0:T(1024)S(1)} %bitcast.29, ...), kind=kOutput, calls=%fused_computation.4 | convolution fusion | flops 59769088 | bytes 5308544 | tf_op jit(solution)/shard_map/dot_general | solution.py:43
  26.9 0.0 copy-start.2
  26.9 6.3 %copy.25 = f32[32,16384]{0,1:T(8,128)} copy(f32[32,16384]{1,0:T(8,128)} %convolution_subtract_fusion) | data formatting | bytes 4194304 | tf_op jit(solution)/shard_map/sub | solution.py:46
  33.1 0.0 collective-permute-done
  33.1 0.0 collective-permute-done.1
  33.1 0.0 copy-done.2
  33.2 8.0 %scatter_custom_fusion = f32[32,16384]{0,1:T(8,128)} fusion(f32[32,16384]{0,1:T(8,128)} %copy.25, s32[128]{0:T(128)S(1)} %compare_select_fusion.1, f32[128]{0:T(128)S(1)} %copy-done.2, f32[32,256]{0,1:T(8,128)S(1)} %pad_maximum_fusion, s32[1024]{0:T(1024)S(1)} %pad_clamp_fusion), kind=kCustom, calls=%fused_computation.14 | custom fusion | flops 8192 | bytes 2232832 | tf_op jit(solution)/shard_map/scatter-add | solution.py:46
  41.2 19.0 %fusion.15 = f32[32,32]{0,1:T(8,128)S(1)} fusion(f32[32,16384]{0,1:T(8,128)} %scatter_custom_fusion), kind=kOutput, calls=%fused_computation.41 | convolution fusion | flops 201326592 | bytes 2101248 | tf_op jit(solution)/shard_map/dot_general | solution.py:47
  60.1 58.2 %psum.7 = f32[32,32]{0,1:T(8,128)S(1)} all-reduce(f32[32,32]{0,1:T(8,128)S(1)} %fusion.15), channel_id=1, replica_groups=mesh['groups'=2,'patch'=16] {'patch'}, use_global_device_ids=true, to_apply=%region_1.2 | all-reduce | flops 1024 | bytes 8192 | tf_op jit(solution)/shard_map/psum | solution.py:50
  118.3 0.1 copy.27
  118.4 2.9 %cholesky.18 = f32[32,32]{1,0:T(8,128)S(1)} custom-call(f32[32,32]{1,0:T(8,128)S(1)} %fusion.9), custom_call_target="Cholesky" | custom-call | tf_op jit(solution)/shard_map/jit(cholesky)/cholesky | solution.py:50
  121.3 0.6 compare_reduce_fusion
  122.0 0.7 select_bitcast_fusion
  122.6 2.4 %custom-call.6 = f32[1,32,32]{1,2,0:T(8,128)S(1)} custom-call(f32[1,32,32]{2,1,0:T(8,128)S(1)} %get-tuple-element.19), custom_call_target="InvertDiagBlocksLowerTriangular" | custom-call | tf_op jit(solution)/shard_map/triangular_solve | solution.py:52
  125.1 12.0 %convolution_multiply_fusion = f32[32,16384]{1,0:T(8,128)} fusion(f32[32,16384]{0,1:T(8,128)} %scatter_custom_fusion, f32[1,32,32]{1,2,0:T(8,128)S(1)} %custom-call.6), kind=kOutput, calls=%fused_computation.3 | convolution fusion | flops 201850880 | bytes 4198400 | tf_op jit(solution)/shard_map/triangular_solve | solution.py:52
  137.1 0.7 copy.28
  (7 shorter events, 0.1 us)
Async XLA Ops:
  0.6 20.5 %copy-start = (f32[8,16384]{1,0:T(8,128)S(1)}, f32[8,16384]{1,0:T(8,128)}, u32[]{:S(2)}) copy-start(f32[8,16384]{1,0:T(8,128)} %param.9) | copy-start | bytes 1572868
  1.4 16.0 %copy-start.3 = (s32[128]{0:T(128)S(1)}, s32[128]{0:T(128)}, u32[]{:S(2)}) copy-start(s32[128]{0:T(128)} %param.13) | copy-start | bytes 1540
  1.4 19.7 %copy-start.1 = (f32[32,16384]{1,0:T(8,128)S(1)}, f32[32,16384]{1,0:T(8,128)}, u32[]{:S(2)}) copy-start(f32[32,16384]{1,0:T(8,128)} %param.8) | copy-start | bytes 6291460
  1.4 19.7 %copy-start.4 = (s32[32]{0:T(128)S(1)}, s32[32]{0:T(128)}, u32[]{:S(2)}) copy-start(s32[32]{0:T(128)} %param.11) | copy-start | bytes 388
  11.8 21.3 %collective-permute-start = (f32[32,64]{0,1:T(8,128)S(1)}, f32[32,64]{0,1:T(8,128)S(1)}, u32[]{:S(2)}, u32[]{:S(2)}) collective-permute-start(f32[32,64]{0,1:T(8,128)S(1)} %get-tuple-element.17), channel_id=1, source_target_pairs={{0,1},{1,2},{2,3},{3,4},{4,5},{5,6},{6,7},{7,8},{8,9},{9,10},{10,1... | collective-permute-start | bytes 24584 | tf_op jit(solution)/shard_map/ppermute | solution.py:14
  12.3 20.8 %collective-permute-start.1 = (f32[32,64]{0,1:T(8,128)S(1)}, f32[32,64]{0,1:T(8,128)S(1)}, u32[]{:S(2)}, u32[]{:S(2)}) collective-permute-start(f32[32,64]{0,1:T(8,128)S(1)} %get-tuple-element.18), channel_id=1, source_target_pairs={{1,0},{2,1},{3,2},{4,3},{5,4},{6,5},{7,6},{8,7},{9,8},{10,9},{11,1... | collective-permute-start | bytes 24584 | tf_op jit(solution)/shard_map/ppermute | solution.py:16
  26.9 6.3 %copy-start.2 = (f32[128]{0:T(128)S(1)}, f32[128]{0:T(128)}, u32[]{:S(2)}) copy-start(f32[128]{0:T(128)} %param.14) | copy-start | bytes 1540
where the time goes:
time: 138 us
  blocking collectives  58.2 us (42%)
  matrix products  36.7 us (27%)
  local copies, waits for them, and re-layouts  21.1 us (15%)
  other arithmetic  15.5 us (11%)
  starting transfers between devices  5.56 us (4%)
    psum x1, blocking collectives, per_device(): lower = jnp.linalg.cholesky(lax.psum(local_gram, 'patch'))  58.2 us
    dot_general x1, matrix products, per_device(): jnp.dot(snapshots, snapshots.T, preferred_element_type=jnp.float32, preci...  19 us
    another operation x1, matrix products, per_device(): lax.linalg.triangular_solve(lower, snapshots, left_side=True, lower=True)  12 us
    scatter-add x1, other arithmetic, per_device(): snapshots = (chosen - banded).at[:, iface_rows].add(coupled)  8.02 us
    unnamed x12, local copies, waits for them, and re-layouts  7.11 us
    sub x1, local copies, waits for them, and re-layouts, per_device(): snapshots = (chosen - banded).at[:, iface_rows].add(coupled)  6.26 us
    dot_general x1, matrix products, per_device(): jnp.dot(one_hot, loads, preferred_element_type=jnp.float32, precision=lax...  5.72 us
    ppermute x1, starting transfers between devices, padded_2(): lax.ppermute(head, axis, [((i + 1) % count, i) for i in range(count)])  5.06 us
  transfers between devices with their start and end apart: 2, of which 0 were waited for; matrix products, arithmetic and copies ran while one was open for 11% of the time, Pallas kernels for 0%

commit v1 on v0

v1 whole, which is shorter than its diff:
```python
import functools
import math

import jax
import jax.numpy as jnp
from jax import lax
from jax.experimental import pallas as pl
from jax.experimental.pallas import tpu as pltpu
from jax.sharding import PartitionSpec as P

LANES = 128
F32 = jnp.float32
BF16 = jnp.bfloat16
VMEM_BYTES = 48 * 1024 * 1024


def halves(x):
    high = x.astype(BF16)
    return high, (x - high.astype(F32)).astype(BF16)


def thirds(x):
    high, rest = x.astype(BF16), None
    rest = x - high.astype(F32)
    mid = rest.astype(BF16)
    return high, mid, (rest - mid.astype(F32)).astype(BF16)


def nt_dot(a, b, precision=None):
    return lax.dot_general(
        a, b, (((1,), (1,)), ((), ())), preferred_element_type=F32, precision=precision
    )


def iota(shape, dim):
    return lax.broadcasted_iota(jnp.int32, shape, dim)


def as_column(row):
    count = row.shape[1]
    wide = jnp.broadcast_to(row.astype(F32), (count, count))
    kept = jnp.where(iota((count, count), 0) == iota((count, count), 1), wide, 0.0)
    return jnp.sum(kept, axis=1, keepdims=True).astype(jnp.int32)


def assemble_kernel(
    n, chunk,
    trial_hbm, loads_hbm, band_hbm, seeds_ref, rows_ref, partner_ref, weight_ref,
    parts_hbm, gram_ref,
    trial_v, loads_v, band_v, snap_v, parts_v, hits_v, own_v, near_v, grams_v,
    in_sem, near_send, near_recv, gram_send, gram_recv, out_sem,
):
    me = lax.axis_index("patch")
    right, left = lax.rem(me + 1, n), lax.rem(me + n - 1, n)
    snaps, count = snap_v.shape
    slots = own_v.shape[1]
    width = band_hbm.shape[0]
    half = (width - 1) // 2
    chunks = count // chunk

    barrier = pltpu.get_barrier_semaphore()

    def greet(d, _):
        pl.semaphore_signal(barrier, inc=1, device_id={"patch": lax.rem(me + d, n)},
                            device_id_type=pl.DeviceIdType.MESH)
        return 0

    get_trial = pltpu.make_async_copy(
        trial_hbm, trial_v.at[:, pl.ds(LANES, count)], in_sem.at[0])
    get_loads = pltpu.make_async_copy(loads_hbm, loads_v, in_sem.at[1])
    get_band = pltpu.make_async_copy(band_hbm, band_v, in_sem.at[2])
    get_trial.start()
    get_loads.start()
    get_band.start()
    lax.fori_loop(1, n, greet, 0)
    trial_v[:, :LANES] = jnp.zeros((snaps, LANES), F32)
    trial_v[:, count + LANES:] = jnp.zeros((snaps, LANES), F32)

    rows_col = as_column(rows_ref[...])

    def mark(c, _):
        at = pl.multiple_of(c * chunk, chunk)
        hit = jnp.where(iota((slots, chunk), 1) == rows_col - at, 1.0, 0.0)
        hits_v[:, pl.ds(at, chunk)] = hit.astype(BF16)
        return 0

    def pick(c, own):
        at = pl.multiple_of(c * chunk, chunk)
        both = jnp.concatenate(halves(trial_v[:, pl.ds(at + LANES, chunk)]), axis=0)
        return own + nt_dot(both, hits_v[:, pl.ds(at, chunk)])

    lax.fori_loop(0, chunks, mark, 0)
    get_trial.wait()
    own = lax.fori_loop(0, chunks, pick, jnp.zeros((2 * snaps, slots), F32))
    own_v[...] = own[:snaps] + own[snaps:]
    pl.semaphore_wait(barrier, n - 1)

    def to_near(side, target):
        return pltpu.make_async_remote_copy(
            src_ref=own_v, dst_ref=near_v.at[side], send_sem=near_send.at[side],
            recv_sem=near_recv.at[side], device_id={"patch": target},
            device_id_type=pl.DeviceIdType.MESH)

    to_right, to_left = to_near(0, right), to_near(1, left)
    to_right.start()
    to_left.start()

    get_loads.wait()
    get_band.wait()
    seeds_col = as_column(seeds_ref[...])
    pattern = iota((snaps, 32), 1)
    chooser = jnp.where(
        ((pattern & 7) == seeds_col) & (pattern < 24), 1.0, 0.0).astype(BF16)

    def build(c, gram):
        at = pl.multiple_of(c * chunk, chunk)
        high, mid, low = thirds(loads_v[:, pl.ds(at, chunk)])
        stacked = jnp.concatenate(
            [high.astype(F32), mid.astype(F32), low.astype(F32), jnp.zeros((8, chunk), F32)], axis=0
        ).astype(BF16)
        chosen = jnp.dot(chooser, stacked, preferred_element_type=F32)
        for g in range(snaps // 8):
            wide = trial_v[g * 8:g * 8 + 8, pl.ds(at, chunk + 2 * LANES)]
            acc = chosen[g * 8:g * 8 + 8]
            for k in range(width):
                shift = (half - k) % (chunk + 2 * LANES)
                moved = pltpu.roll(wide, shift, 1) if shift else wide
                acc = acc - band_v[k:k + 1, pl.ds(at, chunk)] * moved[:, LANES:LANES + chunk]
            snap_v[g * 8:g * 8 + 8, pl.ds(at, chunk)] = acc
        both = jnp.concatenate(halves(snap_v[:, pl.ds(at, chunk)]), axis=0)
        right_side = jnp.concatenate([hits_v[:, pl.ds(at, chunk)], both], axis=0)
        return gram + nt_dot(both, right_side)

    gram = lax.fori_loop(0, chunks, build, jnp.zeros((2 * snaps, slots + 2 * snaps), F32))
    gram = gram[:snaps] + gram[snaps:]
    before = gram[:, :slots]
    gram = gram[:, slots:slots + snaps] + gram[:, slots + snaps:]

    shift_to = jnp.where(
        iota((slots, slots), 0) == jnp.broadcast_to(
            partner_ref[...] & (slots - 1), (slots, slots)), 1.0, 0.0).astype(BF16)
    to_right.wait()
    to_left.wait()
    shared = jnp.where(iota((snaps, slots), 1) < slots // 2, near_v[0], near_v[1])
    sorted_ = jnp.dot(jnp.concatenate(thirds(shared), axis=0), shift_to,
                      preferred_element_type=F32)
    coupled = (sorted_[:snaps] + sorted_[snaps:2 * snaps] + sorted_[2 * snaps:]) * weight_ref[...]
    gram = gram + nt_dot(
        jnp.concatenate([coupled, before], axis=1),
        jnp.concatenate([before + coupled, coupled], axis=1),
        precision=lax.Precision.HIGHEST)

    grams_v[me] = jnp.concatenate([gram[i * 8:i * 8 + 8] for i in range(snaps // 8)], axis=1)

    def to_peer(d):
        return pltpu.make_async_remote_copy(
            src_ref=grams_v.at[me], dst_ref=grams_v.at[me], send_sem=gram_send.at[d],
            recv_sem=gram_recv.at[me], device_id={"patch": lax.rem(me + d, n)},
            device_id_type=pl.DeviceIdType.MESH)

    def from_peer(d):
        peer = lax.rem(me + d, n)
        return pltpu.make_async_remote_copy(
            src_ref=grams_v.at[peer], dst_ref=grams_v.at[peer], send_sem=gram_send.at[d],
            recv_sem=gram_recv.at[peer], device_id={"patch": peer},
            device_id_type=pl.DeviceIdType.MESH)

    def send(d, _):
        to_peer(d).start()
        return 0

    lax.fori_loop(1, n, send, 0)

    coupled_parts = jnp.concatenate(halves(coupled), axis=0)

    def finish(c, _):
        at = pl.multiple_of(c * chunk, chunk)
        added = jnp.dot(coupled_parts, hits_v[:, pl.ds(at, chunk)], preferred_element_type=F32)
        whole = snap_v[:, pl.ds(at, chunk)] + (added[:snaps] + added[snaps:])
        parts_v[:, pl.ds(at, chunk)] = jnp.concatenate(halves(whole), axis=0)
        return 0

    lax.fori_loop(0, chunks, finish, 0)
    put = pltpu.make_async_copy(parts_v, parts_hbm, out_sem)
    put.start()

    def arrive(d, _):
        from_peer(d).wait_recv()
        return 0

    lax.fori_loop(1, n, arrive, 0)
    gram_ref[...] = lax.fori_loop(
        0, n, lambda i, t: t + grams_v[i], jnp.zeros(gram_ref.shape, F32))

    def sent(d, _):
        to_peer(d).wait_send()
        return 0

    lax.fori_loop(1, n, sent, 0)
    put.wait()


def basis_kernel(scale, chunk, gram_ref, parts_hbm, factor_ref, basis_hbm,
                 parts_v, basis_v, in_sem, out_sem):
    snaps, count = basis_v.shape
    get = pltpu.make_async_copy(parts_hbm, parts_v, in_sem)
    get.start()
    packed = gram_ref[...]
    gram = jnp.concatenate(
        [packed[:, i * snaps:(i + 1) * snaps] for i in range(snaps // 8)], axis=0)
    line, lane = iota((snaps, 2 * snaps), 0), iota((snaps, 2 * snaps), 1)
    eye = jnp.where(iota((snaps, snaps), 0) == iota((snaps, snaps), 1), 1.0, 0.0)
    work = jnp.concatenate([gram, eye], axis=1)
    for k in range(snaps - 1):
        column = jnp.broadcast_to(work[:, k:k + 1], work.shape)
        pivot = column[k:k + 1]
        row = work[k:k + 1] / pivot
        work = work - jnp.where(line > k, column, 0.0) * row
    pivots = jnp.sum(jnp.where(line == lane, work, 0.0), axis=1, keepdims=True)
    work = work * lax.rsqrt(pivots)
    upper = jnp.where(lane >= line, work, 0.0)
    factor_ref[...] = upper[:, :snaps] * (1.0 / scale)
    high, mid = halves(work[:, snaps:] * scale)
    high, mid = high.astype(F32), mid.astype(F32)
    inverse = jnp.concatenate(
        [jnp.concatenate([high, high], axis=1), jnp.concatenate([mid, mid], axis=1)], axis=0
    ).astype(BF16)
    get.wait()

    def put(c):
        at = pl.ds(pl.multiple_of(c * chunk, chunk), chunk)
        return pltpu.make_async_copy(basis_v.at[:, at], basis_hbm.at[:, at], out_sem.at[c])

    def step(c, _):
        at = pl.ds(pl.multiple_of(c * chunk, chunk), chunk)
        product = jnp.dot(inverse, parts_v[:, at], preferred_element_type=F32)
        basis_v[:, at] = product[:snaps] + product[snaps:]
        put(c).start()
        return 0

    def done(c, _):
        put(c).wait()
        return 0

    lax.fori_loop(0, count // chunk, step, 0)
    lax.fori_loop(0, count // chunk, done, 0)


def per_device(n, trial, loads, band, seeds, iface_rows, iface_partner, patch_device, iface_weight):
    snaps, count = trial.shape
    slots = iface_rows.shape[0]
    width = band.shape[0]
    chunk = 1024
    any_space = pl.BlockSpec(memory_space=pl.ANY)
    vmem = pl.BlockSpec(memory_space=pltpu.VMEM)
    dma = pltpu.SemaphoreType.DMA
    parts, gram = pl.pallas_call(
        functools.partial(assemble_kernel, n, chunk),
        out_shape=(
            jax.ShapeDtypeStruct((2 * snaps, count), BF16),
            jax.ShapeDtypeStruct((8, LANES), F32),
        ),
        in_specs=[any_space, any_space, any_space, vmem, vmem, vmem, vmem],
        out_specs=(any_space, vmem),
        scratch_shapes=[
            pltpu.VMEM((snaps, count + 2 * LANES), F32),
            pltpu.VMEM(loads.shape, F32),
            pltpu.VMEM(band.shape, F32),
            pltpu.VMEM((snaps, count), F32),
            pltpu.VMEM((2 * snaps, count), BF16),
            pltpu.VMEM((slots, count), BF16),
            pltpu.VMEM((snaps, slots), F32),
            pltpu.VMEM((2, snaps, slots), F32),
            pltpu.VMEM((n, 8, LANES), F32),
            dma((3,)), dma((2,)), dma((2,)), dma((n,)), dma((n,)), dma,
        ],
        compiler_params=pltpu.CompilerParams(
            collective_id=0, has_side_effects=True, vmem_limit_bytes=VMEM_BYTES),
        name="assemble",
    )(trial, loads, band, seeds.reshape(1, snaps), iface_rows.reshape(1, slots),
      iface_partner.reshape(1, slots), iface_weight.reshape(1, slots))
    out_chunk = 2048
    scale = math.sqrt(count * n)
    factor, basis = pl.pallas_call(
        functools.partial(basis_kernel, scale, out_chunk),
        out_shape=(
            jax.ShapeDtypeStruct((snaps, snaps), F32),
            jax.ShapeDtypeStruct((snaps, count), F32),
        ),
        in_specs=[vmem, any_space],
        out_specs=(vmem, any_space),
        scratch_shapes=[
            pltpu.VMEM((2 * snaps, count), BF16),
            pltpu.VMEM((snaps, count), F32),
            dma, dma((count // out_chunk,)),
        ],
        compiler_params=pltpu.CompilerParams(vmem_limit_bytes=VMEM_BYTES),
        name="basis",
    )(gram, parts)
    return factor, basis


def solution(mesh):
    placed = (
        P("groups", "patch"),
        P(None, "patch"),
        P(None, "patch"),
        P("groups"),
        P("patch"),
        P("patch"),
        P(),
        P("patch"),
    )
    return jax.shard_map(
        functools.partial(per_device, mesh.shape["patch"]),
        mesh=mesh,
        in_specs=placed,
        out_specs=(P("groups", None), P("groups", "patch")),
        check_vma=False,
    )
```

time: 138 us -> 35.7 us (0.26)
  blocking collectives: 58.2 us -> 0 us
  matrix products: 36.7 us -> 0 us
  Pallas kernels: 0 us -> 28.3 us
  other arithmetic: 15.5 us -> 0 us
  local copies, waits for them, and re-layouts: 21.1 us -> 6.47 us
  starting transfers between devices: 5.56 us -> 0 us
    psum x1 -> x0, blocking collectives: 58.2 us -> none  [per_device(): lower = jnp.linalg.cholesky(lax.psum(local_gram, 'patch'))]
    pallas_call x0 -> x2, Pallas kernels: none -> 28.3 us  [the longest x1 22.3 us: per_device(): pl.pallas_call(functools.partial(assemble_kernel, n, chunk), out_shape=(j...]
    dot_general x2 -> x0, matrix products: 24.7 us -> none  [the longest x1 19 us: per_device(): jnp.dot(snapshots, snapshots.T, preferred_element_type=jnp.float32, preci...]
    another operation x1 -> x0, matrix products: 12 us -> none  [per_device(): lax.linalg.triangular_solve(lower, snapshots, left_side=True, lower=True)]
    scatter-add x1 -> x0, other arithmetic: 8.02 us -> none  [per_device(): snapshots = (chosen - banded).at[:, iface_rows].add(coupled)]
    another operation x5 -> x0, other arithmetic: 6.68 us -> none  [the longest x3 3.59 us: per_device(): lower = jnp.linalg.cholesky(lax.psum(local_gram, 'patch'))]
    sub x1 -> x0, local copies, waits for them, and re-layouts: 6.26 us -> none  [per_device(): snapshots = (chosen - banded).at[:, iface_rows].add(coupled)]
    ppermute x2 -> x0, starting transfers between devices: 5.56 us -> none  [the longest x1 5.06 us: padded_2(): lax.ppermute(head, axis, [((i + 1) % count, i) for i in range(count)])]
  transfers between devices with their start and end apart: 2 -> 0, of which waited for: 0 -> 0; matrix products, arithmetic and copies ran while one was open for 11% -> 0% of each run, Pallas kernels for 0% -> 0%
where the time goes in v1:
time: 35.7 us; the launch traced here: 35.4 us
  Pallas kernels  28.3 us (79%)
  local copies, waits for them, and re-layouts  6.47 us (18%)
  between operations  0.65 us (2%)
    pallas_call x1, Pallas kernels, per_device(): pl.pallas_call(functools.partial(assemble_kernel, n, chunk), out_shape=(j...  22.3 us
    unnamed x14, local copies, waits for them, and re-layouts  6.47 us
    pallas_call x1, Pallas kernels, per_device(): pl.pallas_call(functools.partial(basis_kernel, scale, out_chunk), out_sha...  5.96 us

profile of v1, /device:TPU:0, one launch (start us, length us, event | category | flops | bytes accessed | tf_op | source)
XLA Modules:
  0.0 35.4 jit_solution(6252162240820432937)
XLA Ops:
  0.6 0.0 copy-start
  0.6 1.6 %copy-done = f32[32,16384]{1,0:T(8,128)S(1)} copy-done((f32[32,16384]{1,0:T(8,128)S(1)}, f32[32,16384]{1,0:T(8,128)}, u32[]{:S(2)}) %copy-start) | copy-done | bytes 2097176
  2.2 0.0 copy-start.1
  2.2 1.2 %copy-done.1 = f32[9,16384]{1,0:T(8,128)S(1)} copy-done((f32[9,16384]{1,0:T(8,128)S(1)}, f32[9,16384]{1,0:T(8,128)}, u32[]{:S(2)}) %copy-start.1) | copy-done | bytes 589848
  3.4 0.0 copy-start.2
  3.5 1.0 %copy-done.2 = f32[8,16384]{1,0:T(8,128)S(1)} copy-done((f32[8,16384]{1,0:T(8,128)S(1)}, f32[8,16384]{1,0:T(8,128)}, u32[]{:S(2)}) %copy-start.2) | copy-done | bytes 524312
  4.5 0.0 copy-start.3
  4.5 0.7 %copy-done.3 = s32[32]{0:T(128)S(1)} copy-done((s32[32]{0:T(128)S(1)}, s32[32]{0:T(128)}, u32[]{:S(2)}) %copy-start.3) | copy-done | bytes 152
  5.1 0.0 copy-start.4
  5.1 0.7 %copy-done.4 = s32[128]{0:T(128)S(1)} copy-done((s32[128]{0:T(128)S(1)}, s32[128]{0:T(128)}, u32[]{:S(2)}) %copy-start.4) | copy-done | bytes 536
  5.8 0.0 copy-start.5
  5.8 0.7 %copy-done.5 = s32[128]{0:T(128)S(1)} copy-done((s32[128]{0:T(128)S(1)}, s32[128]{0:T(128)}, u32[]{:S(2)}) %copy-start.5) | copy-done | bytes 536
  6.5 0.0 copy-start.6
  6.5 0.7 %copy-done.6 = f32[128]{0:T(128)S(1)} copy-done((f32[128]{0:T(128)S(1)}, f32[128]{0:T(128)}, u32[]{:S(2)}) %copy-start.6) | copy-done | bytes 536
  7.1 22.3 %assemble.1 = (bf16[64,16384]{1,0:T(8,128)(2,1)S(1)}, f32[8,128]{1,0:T(8,128)S(1)}) custom-call(f32[32,16384]{1,0:T(8,128)S(1)} %copy-done, f32[8,16384]{1,0:T(8,128)S(1)} %copy-done.2, f32[9,16384]{1,0:T(8,128)S(1)} %copy-done.1, s32[1,32]{1,0:T(1,128)S(1)} %bitcast.4, s32[1,128]{1,0:T(1,128)S(1)} %bitcast.5, s32[1,128]{1,0:T(1,128)S(1)} %bitcast.6, ...), custom_call_target="tpu_custom_call" | custom-call | tf_op jit(solution)/shard_map/assemble/pallas_call | solution.py:257
  29.4 6.0 %basis.1 = (f32[32,32]{1,0:T(8,128)}, f32[32,16384]{1,0:T(8,128)}) custom-call(f32[8,128]{1,0:T(8,128)S(1)} %get-tuple-element.4.gram_ref, bf16[64,16384]{1,0:T(8,128)(2,1)S(1)} %get-tuple-element.5.parts_hbm), custom_call_target="tpu_custom_call" | custom-call | tf_op jit(solution)/shard_map/basis/pallas_call | solution.py:284
Async XLA Ops:
  0.6 1.6 %copy-start = (f32[32,16384]{1,0:T(8,128)S(1)}, f32[32,16384]{1,0:T(8,128)}, u32[]{:S(2)}) copy-start(f32[32,16384]{1,0:T(8,128)} %trial_hbm.1) | copy-start | bytes 6291460
  2.2 1.2 %copy-start.1 = (f32[9,16384]{1,0:T(8,128)S(1)}, f32[9,16384]{1,0:T(8,128)}, u32[]{:S(2)}) copy-start(f32[9,16384]{1,0:T(8,128)} %band_hbm.1) | copy-start | bytes 1769476
  3.4 1.0 %copy-start.2 = (f32[8,16384]{1,0:T(8,128)S(1)}, f32[8,16384]{1,0:T(8,128)}, u32[]{:S(2)}) copy-start(f32[8,16384]{1,0:T(8,128)} %loads_hbm.1) | copy-start | bytes 1572868
  4.5 0.7 %copy-start.3 = (s32[32]{0:T(128)S(1)}, s32[32]{0:T(128)}, u32[]{:S(2)}) copy-start(s32[32]{0:T(128)} %param.11) | copy-start | bytes 388
  5.1 0.7 %copy-start.4 = (s32[128]{0:T(128)S(1)}, s32[128]{0:T(128)}, u32[]{:S(2)}) copy-start(s32[128]{0:T(128)} %param.12) | copy-start | bytes 1540
  5.8 0.7 %copy-start.5 = (s32[128]{0:T(128)S(1)}, s32[128]{0:T(128)}, u32[]{:S(2)}) copy-start(s32[128]{0:T(128)} %param.13) | copy-start | bytes 1540
  6.5 0.7 %copy-start.6 = (f32[128]{0:T(128)S(1)}, f32[128]{0:T(128)}, u32[]{:S(2)}) copy-start(f32[128]{0:T(128)} %param.14) | copy-start | bytes 1540

commit v2 on v1

v2 whole, which is shorter than its diff:
```python
import functools
import math

import jax
import jax.numpy as jnp
from jax import lax
from jax.experimental import pallas as pl
from jax.experimental.pallas import tpu as pltpu
from jax.sharding import PartitionSpec as P

LANES = 128
F32 = jnp.float32
BF16 = jnp.bfloat16
VMEM_BYTES = 60 * 1024 * 1024


def halves(x):
    high = x.astype(BF16)
    return high, (x - high.astype(F32)).astype(BF16)


def thirds(x):
    high, rest = x.astype(BF16), None
    rest = x - high.astype(F32)
    mid = rest.astype(BF16)
    return high, mid, (rest - mid.astype(F32)).astype(BF16)


def nt_dot(a, b, precision=None):
    return lax.dot_general(
        a, b, (((1,), (1,)), ((), ())), preferred_element_type=F32, precision=precision
    )


def iota(shape, dim):
    return lax.broadcasted_iota(jnp.int32, shape, dim)


def as_column(row):
    count = row.shape[1]
    wide = jnp.broadcast_to(row.astype(F32), (count, count))
    kept = jnp.where(iota((count, count), 0) == iota((count, count), 1), wide, 0.0)
    return jnp.sum(kept, axis=1, keepdims=True).astype(jnp.int32)


def assemble_kernel(
    n, chunk, pieces,
    trial_hbm, loads_hbm, band_hbm, seeds_hbm, rows_hbm, partner_hbm, weight_hbm,
    parts_hbm, gram_ref,
    trial_v, loads_v, band_v, turned_v, snap_v, parts_v, seeds_v, rows_v, partner_v, weight_v,
    own_v, near_v, grams_v,
    in_sem, near_send, near_recv, gram_send, gram_recv, out_sem,
):
    me = lax.axis_index("patch")
    right, left = lax.rem(me + 1, n), lax.rem(me + n - 1, n)
    snaps, count = snap_v.shape
    slots = own_v.shape[1]
    width = band_hbm.shape[0]
    piece = count // pieces
    wide_count = count + 2 * LANES

    barrier = pltpu.get_barrier_semaphore()

    def greet(d, _):
        pl.semaphore_signal(barrier, inc=1, device_id={"patch": lax.rem(me + d, n)},
                            device_id_type=pl.DeviceIdType.MESH)
        return 0

    inside = pl.ds(LANES, count)
    get_rows = pltpu.make_async_copy(rows_hbm, rows_v, in_sem.at[0])
    get_band = pltpu.make_async_copy(band_hbm, band_v.at[:, inside], in_sem.at[1])
    get_loads = pltpu.make_async_copy(loads_hbm, loads_v, in_sem.at[2])
    get_seeds = pltpu.make_async_copy(seeds_hbm, seeds_v, in_sem.at[3])
    get_partner = pltpu.make_async_copy(partner_hbm, partner_v, in_sem.at[4])
    get_weight = pltpu.make_async_copy(weight_hbm, weight_v, in_sem.at[5])
    get_trial = [
        pltpu.make_async_copy(
            trial_hbm.at[:, pl.ds(p * piece, piece)],
            trial_v.at[:, pl.ds(LANES + p * piece, piece)], in_sem.at[6 + p])
        for p in range(pieces)
    ]
    for copy in [get_rows, get_band] + get_trial + [get_loads, get_seeds, get_partner, get_weight]:
        copy.start()
    lax.fori_loop(1, n, greet, 0)
    for edge in (0, count + LANES):
        trial_v[:, edge:edge + LANES] = jnp.zeros((snaps, LANES), F32)
        band_v[:, edge:edge + LANES] = jnp.zeros((width, LANES), F32)

    get_rows.wait()
    get_band.wait()
    first = band_v[0:8, :]
    line = iota((8, wide_count), 0)
    turned_v[0:8, :] = jnp.where(
        line < 3, pltpu.roll(first, wide_count - 3, 1),
        jnp.where(line < 6, first, pltpu.roll(first, 3, 1)))
    turned_v[8:9, :] = pltpu.roll(band_v[8:9, :], 3, 1)

    rows = rows_v[...]

    def hits(at, size):
        return jnp.where(iota((size, slots), 0) == rows - at, 1.0, 0.0).astype(BF16)

    own = jnp.zeros((2 * snaps, slots), F32)
    for p in range(pieces):
        get_trial[p].wait()
        both = jnp.concatenate(
            halves(trial_v[:, LANES + p * piece:LANES + (p + 1) * piece]), axis=0)
        own = own + jnp.dot(both, hits(p * piece, piece), preferred_element_type=F32)
    own_v[...] = own[:snaps] + own[snaps:]
    pl.semaphore_wait(barrier, n - 1)

    def to_near(side, target):
        return pltpu.make_async_remote_copy(
            src_ref=own_v, dst_ref=near_v.at[side], send_sem=near_send.at[side],
            recv_sem=near_recv.at[side], device_id={"patch": target},
            device_id_type=pl.DeviceIdType.MESH)

    to_right, to_left = to_near(0, right), to_near(1, left)
    to_right.start()
    to_left.start()

    for copy in (get_loads, get_seeds, get_partner, get_weight):
        copy.wait()
    seeds_col = as_column(seeds_v[...])
    pattern = iota((snaps, 32), 1)
    chooser = jnp.where(
        ((pattern & 7) == seeds_col) & (pattern < 24), 1.0, 0.0).astype(BF16)

    span = chunk + 2 * LANES
    gram = jnp.zeros((2 * snaps, 2 * snaps), F32)
    before = jnp.zeros((2 * snaps, slots), F32)
    for c in range(count // chunk):
        at = c * chunk
        high, mid, low = thirds(loads_v[:, at:at + chunk])
        stacked = jnp.concatenate(
            [high.astype(F32), mid.astype(F32), low.astype(F32), jnp.zeros((8, chunk), F32)], axis=0
        ).astype(BF16)
        chosen = jnp.dot(chooser, stacked, preferred_element_type=F32)
        for g in range(snaps // 8):
            here = trial_v[g * 8:g * 8 + 8, at:at + span]
            behind, ahead = pltpu.roll(here, 1, 1), pltpu.roll(here, span - 1, 1)
            acc = chosen[g * 8:g * 8 + 8]
            for far in (-1, 0, 1):
                k = 3 * far + 4
                term = (turned_v[k - 1:k, at:at + span] * behind
                        + turned_v[k:k + 1, at:at + span] * here
                        + turned_v[k + 1:k + 2, at:at + span] * ahead)
                if far:
                    term = pltpu.roll(term, (-3 * far) % span, 1)
                acc = acc - term[:, LANES:LANES + chunk]
            snap_v[g * 8:g * 8 + 8, at:at + chunk] = acc
        both = jnp.concatenate(halves(snap_v[:, at:at + chunk]), axis=0)
        gram = gram + nt_dot(both, both)
        before = before + jnp.dot(both, hits(at, chunk), preferred_element_type=F32)
    gram = gram[:snaps] + gram[snaps:]
    gram = gram[:, :snaps] + gram[:, snaps:]
    before = before[:snaps] + before[snaps:]

    order = jnp.where(
        iota((slots, slots), 0) == (partner_v[...] & (slots - 1)), 1.0, 0.0).astype(BF16)
    to_right.wait()
    to_left.wait()
    shared = jnp.where(iota((snaps, slots), 1) < slots // 2, near_v[0], near_v[1])
    coupled = jnp.dot(jnp.concatenate(thirds(shared), axis=0), order, preferred_element_type=F32)
    coupled = (coupled[:snaps] + coupled[snaps:2 * snaps] + coupled[2 * snaps:]) * weight_v[...]
    gram = gram + nt_dot(
        jnp.concatenate([coupled, before], axis=1),
        jnp.concatenate([before + coupled, coupled], axis=1),
        precision=lax.Precision.HIGHEST)

    grams_v[me] = jnp.concatenate([gram[i * 8:i * 8 + 8] for i in range(snaps // 8)], axis=1)

    def to_peer(d):
        return pltpu.make_async_remote_copy(
            src_ref=grams_v.at[me], dst_ref=grams_v.at[me], send_sem=gram_send.at[d],
            recv_sem=gram_recv.at[me], device_id={"patch": lax.rem(me + d, n)},
            device_id_type=pl.DeviceIdType.MESH)

    def from_peer(d):
        peer = lax.rem(me + d, n)
        return pltpu.make_async_remote_copy(
            src_ref=grams_v.at[peer], dst_ref=grams_v.at[peer], send_sem=gram_send.at[d],
            recv_sem=gram_recv.at[peer], device_id={"patch": peer},
            device_id_type=pl.DeviceIdType.MESH)

    def send(d, _):
        to_peer(d).start()
        return 0

    lax.fori_loop(1, n, send, 0)

    rows_col = as_column(rows)
    coupled_parts = jnp.concatenate(halves(coupled), axis=0)
    puts = []
    for p in range(pieces):
        at = p * piece
        hit = jnp.where(iota((slots, piece), 1) == rows_col - at, 1.0, 0.0).astype(BF16)
        added = jnp.dot(coupled_parts, hit, preferred_element_type=F32)
        whole = snap_v[:, at:at + piece] + (added[:snaps] + added[snaps:])
        parts_v[:, at:at + piece] = jnp.concatenate(halves(whole), axis=0)
        cut = pl.ds(at, piece)
        puts.append(pltpu.make_async_copy(parts_v.at[:, cut], parts_hbm.at[:, cut], out_sem.at[p]))
        puts[p].start()

    def arrive(d, _):
        from_peer(d).wait_recv()
        return 0

    lax.fori_loop(1, n, arrive, 0)
    gram_ref[...] = lax.fori_loop(
        0, n, lambda i, t: t + grams_v[i], jnp.zeros(gram_ref.shape, F32))

    def sent(d, _):
        to_peer(d).wait_send()
        return 0

    lax.fori_loop(1, n, sent, 0)
    for put in puts:
        put.wait()


def basis_kernel(scale, chunk, gram_ref, parts_hbm, factor_ref, basis_hbm,
                 parts_v, basis_v, in_sem, out_sem):
    snaps, count = basis_v.shape
    get = pltpu.make_async_copy(parts_hbm, parts_v, in_sem)
    get.start()
    packed = gram_ref[...]
    gram = jnp.concatenate(
        [packed[:, i * snaps:(i + 1) * snaps] for i in range(snaps // 8)], axis=0)
    line, lane = iota((snaps, 2 * snaps), 0), iota((snaps, 2 * snaps), 1)
    eye = jnp.where(iota((snaps, snaps), 0) == iota((snaps, snaps), 1), 1.0, 0.0)
    work = jnp.concatenate([gram, eye], axis=1)
    for k in range(0, snaps, 2):
        column0 = jnp.broadcast_to(work[:, k:k + 1], work.shape)
        column1 = jnp.broadcast_to(work[:, k + 1:k + 2], work.shape)
        row0 = work[k:k + 1]
        inverse0 = 1.0 / column0[k:k + 1]
        share = column0[k + 1:k + 2] * inverse0
        row1 = work[k + 1:k + 2] - share * row0
        inverse1 = 1.0 / (column1[k + 1:k + 2] - share * column1[k:k + 1])
        column1 = column1 - column0 * (column1[k:k + 1] * inverse0)
        work = (work - jnp.where(line > k, column0, 0.0) * (row0 * inverse0)
                - jnp.where(line > k + 1, column1, 0.0) * (row1 * inverse1))
    pivots = jnp.sum(jnp.where(line == lane, work, 0.0), axis=1, keepdims=True)
    work = work * lax.rsqrt(pivots)
    upper = jnp.where(lane >= line, work, 0.0)
    factor_ref[...] = upper[:, :snaps] * (1.0 / scale)
    high, mid = halves(work[:, snaps:] * scale)
    high, mid = high.astype(F32), mid.astype(F32)
    inverse = jnp.concatenate(
        [jnp.concatenate([high, high], axis=1), jnp.concatenate([mid, mid], axis=1)], axis=0
    ).astype(BF16)
    get.wait()
    puts = []
    for c in range(count // chunk):
        at = pl.ds(c * chunk, chunk)
        product = jnp.dot(inverse, parts_v[:, at], preferred_element_type=F32)
        basis_v[:, at] = product[:snaps] + product[snaps:]
        puts.append(pltpu.make_async_copy(basis_v.at[:, at], basis_hbm.at[:, at], out_sem.at[c]))
        puts[c].start()
    for put in puts:
        put.wait()


def per_device(n, trial, loads, band, seeds, iface_rows, iface_partner, patch_device, iface_weight):
    snaps, count = trial.shape
    slots = iface_rows.shape[0]
    width = band.shape[0]
    chunk, pieces, out_chunk = 1024, 4, 4096
    hbm = pl.BlockSpec(memory_space=pltpu.HBM)
    vmem = pl.BlockSpec(memory_space=pltpu.VMEM)
    dma = pltpu.SemaphoreType.DMA
    parts, gram = pl.pallas_call(
        functools.partial(assemble_kernel, n, chunk, pieces),
        out_shape=(
            jax.ShapeDtypeStruct((2 * snaps, count), BF16),
            jax.ShapeDtypeStruct((8, LANES), F32),
        ),
        in_specs=[hbm] * 7,
        out_specs=(hbm, vmem),
        scratch_shapes=[
            pltpu.VMEM((snaps, count + 2 * LANES), F32),
            pltpu.VMEM(loads.shape, F32),
            pltpu.VMEM((width, count + 2 * LANES), F32),
            pltpu.VMEM((width, count + 2 * LANES), F32),
            pltpu.VMEM((snaps, count), F32),
            pltpu.VMEM((2 * snaps, count), BF16),
            pltpu.VMEM((1, snaps), jnp.int32),
            pltpu.VMEM((1, slots), jnp.int32),
            pltpu.VMEM((1, slots), jnp.int32),
            pltpu.VMEM((1, slots), F32),
            pltpu.VMEM((snaps, slots), F32),
            pltpu.VMEM((2, snaps, slots), F32),
            pltpu.VMEM((n, 8, LANES), F32),
            dma((6 + pieces,)), dma((2,)), dma((2,)), dma((n,)), dma((n,)),
            dma((pieces,)),
        ],
        compiler_params=pltpu.CompilerParams(
            collective_id=0, has_side_effects=True, vmem_limit_bytes=VMEM_BYTES),
        name="assemble",
    )(trial, loads, band, seeds.reshape(1, snaps), iface_rows.reshape(1, slots),
      iface_partner.reshape(1, slots), iface_weight.reshape(1, slots))
    scale = math.sqrt(count * n)
    factor, basis = pl.pallas_call(
        functools.partial(basis_kernel, scale, out_chunk),
        out_shape=(
            jax.ShapeDtypeStruct((snaps, snaps), F32),
            jax.ShapeDtypeStruct((snaps, count), F32),
        ),
        in_specs=[vmem, hbm],
        out_specs=(vmem, hbm),
        scratch_shapes=[
            pltpu.VMEM((2 * snaps, count), BF16),
            pltpu.VMEM((snaps, count), F32),
            dma, dma((count // out_chunk,)),
        ],
        compiler_params=pltpu.CompilerParams(vmem_limit_bytes=VMEM_BYTES),
        name="basis",
    )(gram, parts)
    return factor, basis


def solution(mesh):
    placed = (
        P("groups", "patch"),
        P(None, "patch"),
        P(None, "patch"),
        P("groups"),
        P("patch"),
        P("patch"),
        P(),
        P("patch"),
    )
    return jax.shard_map(
        functools.partial(per_device, mesh.shape["patch"]),
        mesh=mesh,
        in_specs=placed,
        out_specs=(P("groups", None), P("groups", "patch")),
        check_vma=False,
    )
```

time: 35.7 us -> 21.9 us (0.61)
  Pallas kernels: 28.3 us -> 21.1 us
  local copies, waits for them, and re-layouts: 6.47 us -> 0 us
    unnamed x14 -> x0, local copies, waits for them, and re-layouts: 6.47 us -> none
    pallas_call x1, Pallas kernels: 22.3 us -> 16.4 us  [per_device(): pl.pallas_call(functools.partial(assemble_kernel, n, chunk, pieces), out_...]
    pallas_call x1, Pallas kernels: 5.96 us -> 4.68 us  [per_device(): pl.pallas_call(functools.partial(basis_kernel, scale, out_chunk), out_sha...]
where the time goes in v2:
time: 21.9 us; the launch traced here: 21.8 us
  Pallas kernels  21.1 us (96%)
  between operations  0.64 us (3%)
    pallas_call x1, Pallas kernels, per_device(): pl.pallas_call(functools.partial(assemble_kernel, n, chunk, pieces), out_...  16.4 us
    pallas_call x1, Pallas kernels, per_device(): pl.pallas_call(functools.partial(basis_kernel, scale, out_chunk), out_sha...  4.68 us

profile of v2, /device:TPU:0, one launch (start us, length us, event | category | flops | bytes accessed | tf_op | source)
XLA Modules:
  0.0 21.8 jit_solution(1376484116889420733)
XLA Ops:
  0.6 16.4 %assemble.1 = (bf16[64,16384]{1,0:T(8,128)(2,1)}, f32[8,128]{1,0:T(8,128)}) custom-call(f32[32,16384]{1,0:T(8,128)} %trial_hbm.1, f32[8,16384]{1,0:T(8,128)} %loads_hbm.1, f32[9,16384]{1,0:T(8,128)} %band_hbm.1, s32[1,32]{1,0:T(1,128)} %bitcast.4, s32[1,128]{1,0:T(1,128)} %bitcast.5, s32[1,128]{1,0:T(1,128)} %bitcast.6, f32[1,128]{1,0:T(1,128)} %bitcast.7), custom_call_target="tpu_custom_call" | custom-call | tf_op jit(solution)/shard_map/assemble/pallas_call | solution.py:273
  17.1 4.7 %basis.1 = (f32[32,32]{1,0:T(8,128)}, f32[32,16384]{1,0:T(8,128)}) custom-call(f32[8,128]{1,0:T(8,128)} %get-tuple-element.4.gram_ref, bf16[64,16384]{1,0:T(8,128)(2,1)} %get-tuple-element.5.parts_hbm), custom_call_target="tpu_custom_call" | custom-call | tf_op jit(solution)/shard_map/basis/pallas_call | solution.py:304

commit v3 on v2

--- a/solution.py
+++ b/solution.py
@@ -207,8 +207,10 @@
         return 0
 
     lax.fori_loop(1, n, arrive, 0)
-    gram_ref[...] = lax.fori_loop(
-        0, n, lambda i, t: t + grams_v[i], jnp.zeros(gram_ref.shape, F32))
+    total = grams_v[0]
+    for i in range(1, n):
+        total = total + grams_v[i]
+    gram_ref[...] = total
 
     def sent(d, _):
         to_peer(d).wait_send()
@@ -219,7 +221,7 @@
         put.wait()
 
 
-def basis_kernel(scale, chunk, gram_ref, parts_hbm, factor_ref, basis_hbm,
+def basis_kernel(scale, chunk, block, gram_ref, parts_hbm, factor_ref, basis_hbm,
                  parts_v, basis_v, in_sem, out_sem):
     snaps, count = basis_v.shape
     get = pltpu.make_async_copy(parts_hbm, parts_v, in_sem)
@@ -230,17 +232,14 @@
     line, lane = iota((snaps, 2 * snaps), 0), iota((snaps, 2 * snaps), 1)
     eye = jnp.where(iota((snaps, snaps), 0) == iota((snaps, snaps), 1), 1.0, 0.0)
     work = jnp.concatenate([gram, eye], axis=1)
-    for k in range(0, snaps, 2):
-        column0 = jnp.broadcast_to(work[:, k:k + 1], work.shape)
-        column1 = jnp.broadcast_to(work[:, k + 1:k + 2], work.shape)
-        row0 = work[k:k + 1]
-        inverse0 = 1.0 / column0[k:k + 1]
-        share = column0[k + 1:k + 2] * inverse0
-        row1 = work[k + 1:k + 2] - share * row0
-        inverse1 = 1.0 / (column1[k + 1:k + 2] - share * column1[k:k + 1])
-        column1 = column1 - column0 * (column1[k:k + 1] * inverse0)
-        work = (work - jnp.where(line > k, column0, 0.0) * (row0 * inverse0)
-                - jnp.where(line > k + 1, column1, 0.0) * (row1 * inverse1))
+    for k in range(0, snaps, block):
+        columns = [jnp.broadcast_to(work[:, k + j:k + j + 1], work.shape) for j in range(block)]
+        for j in range(block):
+            m = k + j
+            inverse = 1.0 / columns[j][m:m + 1]
+            work = work - jnp.where(line > m, columns[j], 0.0) * (work[m:m + 1] * inverse)
+            for i in range(j + 1, block):
+                columns[i] = columns[i] - columns[j] * (columns[i][m:m + 1] * inverse)
     pivots = jnp.sum(jnp.where(line == lane, work, 0.0), axis=1, keepdims=True)
     work = work * lax.rsqrt(pivots)
     upper = jnp.where(lane >= line, work, 0.0)
@@ -266,7 +265,7 @@
     snaps, count = trial.shape
     slots = iface_rows.shape[0]
     width = band.shape[0]
-    chunk, pieces, out_chunk = 1024, 4, 4096
+    chunk, pieces, out_chunk = 1024, 2, 4096
     hbm = pl.BlockSpec(memory_space=pltpu.HBM)
     vmem = pl.BlockSpec(memory_space=pltpu.VMEM)
     dma = pltpu.SemaphoreType.DMA
@@ -302,7 +301,7 @@
       iface_partner.reshape(1, slots), iface_weight.reshape(1, slots))
     scale = math.sqrt(count * n)
     factor, basis = pl.pallas_call(
-        functools.partial(basis_kernel, scale, out_chunk),
+        functools.partial(basis_kernel, scale, out_chunk, 16),
         out_shape=(
             jax.ShapeDtypeStruct((snaps, snaps), F32),
             jax.ShapeDtypeStruct((snaps, count), F32),

time: 21.9 us -> 21.8 us (level)
  no operation moved by 1% of the time
where the time goes in v3:
time: 21.8 us; the launch traced here: 21.6 us
  Pallas kernels  21 us (96%)
  between operations  0.64 us (3%)
    pallas_call x1, Pallas kernels, per_device(): pl.pallas_call(functools.partial(assemble_kernel, n, chunk, pieces), out_...  16.5 us
    pallas_call x1, Pallas kernels, per_device(): pl.pallas_call(functools.partial(basis_kernel, scale, out_chunk, 16), out...  4.52 us

profile of v3, /device:TPU:0, one launch (start us, length us, event | category | flops | bytes accessed | tf_op | source)
XLA Modules:
  0.0 21.6 jit_solution(15562517668222205086)
XLA Ops:
  0.6 16.5 %assemble.1 = (bf16[64,16384]{1,0:T(8,128)(2,1)}, f32[8,128]{1,0:T(8,128)}) custom-call(f32[32,16384]{1,0:T(8,128)} %trial_hbm.1, f32[8,16384]{1,0:T(8,128)} %loads_hbm.1, f32[9,16384]{1,0:T(8,128)} %band_hbm.1, s32[1,32]{1,0:T(1,128)} %bitcast.4, s32[1,128]{1,0:T(1,128)} %bitcast.5, s32[1,128]{1,0:T(1,128)} %bitcast.6, f32[1,128]{1,0:T(1,128)} %bitcast.7), custom_call_target="tpu_custom_call" | custom-call | tf_op jit(solution)/shard_map/assemble/pallas_call | solution.py:272
  17.1 4.5 %basis.1 = (f32[32,32]{1,0:T(8,128)}, f32[32,16384]{1,0:T(8,128)}) custom-call(f32[8,128]{1,0:T(8,128)} %get-tuple-element.4.gram_ref, bf16[64,16384]{1,0:T(8,128)(2,1)} %get-tuple-element.5.parts_hbm), custom_call_target="tpu_custom_call" | custom-call | tf_op jit(solution)/shard_map/basis/pallas_call | solution.py:303
